TPU v7x, 32 devices: a whole 2x2x4 slice. The times are simulated.
32 devices in a mesh: feat: 8 (over y, x, core), node: 4 (over z).
Axes of the slice: x: 2, y: 2, z: 4, core: 2. Of those that a mesh axis runs over, the one named last changes fastest.
Arguments:
- features: bfloat16 [4, 512, 16384], P('node', 'feat'), may hold values from -6 to 6
- target_ids: int32 [4, 4096], P('node'), may hold values from 0 to 16383
- block_ids: int32 [4, 32, 8], P('node'), may hold values from 0 to 127
- tile_counts: int32 [4, 32], P('node'), may hold values from 1 to 8, as said below
- adjacency: bfloat16 [4, 32, 8, 128, 128], P('node'), may hold values from 0 to 0.25
- w_neigh: bfloat16 [256, 512], P(None, 'feat'), may hold values from -0.1875 to 0.1875
- w_self: bfloat16 [256, 512], P(None, 'feat'), may hold values from -0.1875 to 0.1875
- w_head: bfloat16 [256, 256], replicated, may hold values from -0.375 to 0.375
- grad_scores: bfloat16 [4, 4096, 256], P('node', 'feat'), may hold values from -6 to 6
Outputs:
- scores: bfloat16 [4, 4096, 256], P('node', 'feat')
- grad_head: float32 [256, 256], replicated
- grad_neigh: float32 [256, 512], P(None, 'feat')
- grad_self: float32 [256, 512], P(None, 'feat')
Inputs may be any that keep to these rules, and one draw needn't show every extreme that they name: `tile_counts`: one group, drawn from the seed, has all of its tiles at 8 live slots; every tile of the other groups has fewer than 8.
All inputs are finite; a program needn't handle non-finite values.
Results may differ from a plain program's by a relative error of at most 0.0056.
Values may be sent and summed in bfloat16 or wider, within the bound.
A program may use at most 64 MiB of HBM per device.

v0:
```python
import jax
import jax.numpy as jnp
from jax import lax
from jax.sharding import PartitionSpec as P


def aggregate_local(feature_rows, block_row, count_row, adjacency_group):
    width = feature_rows.shape[0]
    tiles = block_row.shape[0]
    slots = block_row.shape[1]
    blocks = feature_rows.reshape(width, -1, 128)
    gathered = jnp.take(blocks, block_row.reshape(-1), axis=1).reshape(width, tiles, slots, 128)
    live = (jnp.arange(slots, dtype=jnp.int32)[None, :] < count_row[:, None]).astype(jnp.bfloat16)
    masked = gathered * live[None, :, :, None]
    summed = jnp.einsum(
        "tkrs,ftks->ftr", adjacency_group, masked, preferred_element_type=jnp.float32
    )
    summed = summed / count_row.astype(jnp.float32)[None, :, None]
    return summed.astype(jnp.bfloat16).reshape(width, tiles * 128)


def contract_first(left, right):
    return lax.dot_general(
        left, right, (((0,), (1,)), ((), ())), preferred_element_type=jnp.float32
    )


def body(
    features, target_ids, block_ids, tile_counts, adjacency, w_neigh, w_self, w_head, grad_scores
):
    feature_rows = features[0]
    aggregate = aggregate_local(feature_rows, block_ids[0], tile_counts[0], adjacency[0])
    own = jnp.take(feature_rows, target_ids[0], axis=1)
    agg_part = aggregate
    own_part = own
    preact = lax.psum_scatter(
        contract_first(agg_part, w_neigh) + contract_first(own_part, w_self),
        "feat",
        scatter_dimension=0,
        tiled=True,
    )
    hidden = jax.nn.silu(preact).astype(jnp.bfloat16)
    scores = jnp.dot(hidden, w_head.T, preferred_element_type=jnp.float32).astype(jnp.bfloat16)
    cotangent = grad_scores[0]
    head_local = lax.dot_general(
        cotangent, hidden, (((0,), (0,)), ((), ())), preferred_element_type=jnp.float32
    )
    grad_head = lax.psum(head_local, ("feat", "node"))
    grad_hidden = jnp.dot(cotangent, w_head, preferred_element_type=jnp.float32)
    sigma = jax.nn.sigmoid(preact)
    grad_pre = (grad_hidden * sigma * (1.0 + preact * (1.0 - sigma))).astype(jnp.bfloat16)
    shard_piece = lax.all_gather(grad_pre, "feat", axis=0, tiled=True)
    agg_part = aggregate
    own_part = own
    neigh_local = contract_first(shard_piece, agg_part)
    self_local = contract_first(shard_piece, own_part)
    grad_neigh, grad_self = lax.psum((neigh_local, self_local), "node")
    return (scores[None], grad_head, grad_neigh, grad_self)


def solution(mesh):
    in_specs = (
        P("node", "feat", None),
        P("node", None),
        P("node", None, None),
        P("node", None),
        P("node", None, None, None, None),
        P(None, "feat"),
        P(None, "feat"),
        P(),
        P("node", "feat", None),
    )
    out_specs = (P("node", "feat", None), P(), P(None, "feat"), P(None, "feat"))
    return jax.shard_map(body, mesh=mesh, in_specs=in_specs, out_specs=out_specs, check_vma=False)
```

profile of v0, /device:TPU:0, one launch (start us, length us, event | category | flops | bytes accessed | tf_op | source)
XLA Modules:
  0.0 308.8 jit_solution(13335983999297234126)
XLA Ops:
  7.2 0.8 compare_and_fusion.1
  8.1 0.8 copy.23
  9.6 0.7 compare_select_fusion
  10.3 0.7 compare_and_fusion
  11.1 0.7 fusion.33
  11.9 4.8 %copy.26 = bf16[1,64,16384]{1,2,0:T(8,128)(2,1)} copy(bf16[1,64,16384]{2,1,0:T(8,128)(2,1)} %param.9) | data formatting | bytes 4194304 | tf_op args[0]
  17.3 1.4 copy.24
  18.6 3.1 gather_fusion
  21.7 13.8 %gather_fusion.1 = bf16[4096,64]{1,0:T(8,128)(2,1)S(1)} fusion(bf16[64,16384]{0,1:T(8,128)(2,1)} %bitcast.57, s32[4096]{0:T(1024)S(1)} %broadcast_clamp_fusion), kind=kCustom, calls=%fused_computation.1 | custom fusion | bytes 1064960 | tf_op jit(solution)/shard_map/jit(_take)/gather | solution.py:33
  35.5 1.5 fusion.29
  37.7 5.7 %fusion.19 = bf16[32,8,8,128]{3,2,1,0:T(8,128)(2,1)S(1)} fusion(bf16[1,32,8,128,128]{4,3,2,1,0:T(8,128)(2,1)} %param.13, bf16[64,32,8,128]{3,0,2,1:T(8,128)(2,1)S(1)} %bitcast.60, pred[32,8]{1,0:T(8,128)(4,1)S(1)} %copy.22, bf16[32,8]{1,0:T(8,128)(2,1)S(1)} %fusion.33, f32[32]{0:T(128)S(1)} %bitcast_convert_fusion), kind=kOutput, calls=%fused_computation.19 | convolution fusion | flops 541589504 | bytes 13108096 | tf_op jit(solution)/shard_map/tkrs,ftks->ftr/dot_general | solution.py:15
  43.4 2.7 convolution_add_fusion
  46.2 54.1 %reduce-scatter.2.cloned.1.call-done = f32[512,256]{1,0:T(8,128)} async-done(((f32[4096,256]{1,0:T(8,128)}), f32[512,256]{1,0:T(8,128)}) %reduce-scatter.2.cloned.1.call-update) | async-done | bytes 524304 | tf_op jit(solution)/shard_map/reduce_scatter | solution.py:36
  100.3 2.0 fusion.13
  102.4 2.1 convolution_bitcast_fusion
  104.6 26.3 %all-gather.2.cloned.1.call-done = bf16[4096,256]{1,0:T(8,128)(2,1)} async-done(((bf16[512,256]{1,0:T(8,128)(2,1)}), bf16[4096,256]{1,0:T(8,128)(2,1)}) %all-gather.2.cloned.1.call-update) | async-done | bytes 2097168 | tf_op jit(solution)/shard_map/all_gather | solution.py:52
  130.9 4.9 %fusion.30 = f32[256,64]{0,1:T(8,128)} fusion(bf16[4096,256]{1,0:T(8,128)(2,1)} %all-gather.2.cloned.1.call-done, bf16[4096,64]{1,0:T(8,128)(2,1)S(1)} %gather_fusion.1, pred[4096]{0:T(1024)(128)(4,1)S(1)} %compare_and_fusion), kind=kOutput, calls=%fused_computation.28 | convolution fusion | flops 134479872 | bytes 2691072 | tf_op jit(solution)/shard_map/dot_general | solution.py:23
  135.8 1.1 fusion.24
  136.9 1.0 fusion.14
  137.9 124.9 %all-reduce.4.cloned.1.call-done = f32[256,256]{0,1:T(8,128)} async-done(((f32[256,256]{0,1:T(8,128)}), f32[256,256]{0,1:T(8,128)}) %all-reduce.4.cloned.1.call-update) | async-done | bytes 262160 | tf_op jit(solution)/shard_map/psum | solution.py:48
  262.9 1.8 copy.27
  264.6 34.7 %all-reduce.6.cloned.1.call-done = (f32[256,64]{0,1:T(8,128)}, f32[256,64]{0,1:T(8,128)}) async-done(((f32[256,64]{0,1:T(8,128)}, f32[256,64]{0,1:T(8,128)}), (f32[256,64]{0,1:T(8,128)}, f32[256,64]{0,1:T(8,128)})) %all-reduce.6.cloned.1.call-update) | async-done | bytes 131088 | tf_op jit(solution)/shard_map/psum | solution.py:57
  299.4 1.5 copy.42
  300.8 1.5 copy.43
  (31 shorter events, 2.4 us)
Async XLA Ops:
  7.2 93.1 %copy-start = (bf16[1,512,256]{2,1,0:T(8,128)(2,1)S(1)}, bf16[1,512,256]{2,1,0:T(8,128)(2,1)}, u32[]{:S(2)}) copy-start(bf16[1,512,256]{2,1,0:T(8,128)(2,1)} %param.17) | copy-start | bytes 786436
  7.2 9.5 %copy-start.1 = (bf16[1,64,16384]{2,1,0:T(8,128)(2,1)S(1)}, bf16[1,64,16384]{2,1,0:T(8,128)(2,1)}, u32[]{:S(2)}) copy-start(bf16[1,64,16384]{2,1,0:T(8,128)(2,1)} %param.9) | copy-start | bytes 6291460
  7.2 93.1 %reduce-scatter.2.cloned.1.call-start = ((), (), s32[]{:S(2)}) async-start(), calls=%async_computation.1 | async-start | bytes 4718592 | tf_op jit(solution)/shard_map/reduce_scatter | solution.py:36
  21.7 13.8 %copy-start.4 = (bf16[256,64]{0,1:T(8,128)(2,1)S(1)}, bf16[256,64]{0,1:T(8,128)(2,1)}, u32[]{:S(2)}) copy-start(bf16[256,64]{0,1:T(8,128)(2,1)} %param.15) | copy-start | bytes 98308
  35.5 2.2 copy-start.2
  37.7 5.7 %copy-start.5 = (bf16[256,64]{0,1:T(8,128)(2,1)S(1)}, bf16[256,64]{0,1:T(8,128)(2,1)}, u32[]{:S(2)}) copy-start(bf16[256,64]{0,1:T(8,128)(2,1)} %param.14) | copy-start | bytes 98308
  46.1 54.2 %copy-start.7 = (bf16[256,256]{1,0:T(8,128)(2,1)S(1)}, bf16[256,256]{1,0:T(8,128)(2,1)}, u32[]{:S(2)}) copy-start(bf16[256,256]{1,0:T(8,128)(2,1)} %param.16) | copy-start | bytes 393220
  46.1 84.7 %all-gather.2.cloned.1.call-start = ((), (), s32[]{:S(2)}) async-start(), calls=%async_computation.3 | async-start | bytes 2359296 | tf_op jit(solution)/shard_map/all_gather | solution.py:52
  102.4 160.5 %all-reduce.4.cloned.1.call-start = ((), (), s32[]{:S(2)}) async-start(), calls=%async_computation.2 | async-start | bytes 524288 | tf_op jit(solution)/shard_map/psum | solution.py:48
  104.5 32.5 %copy-start.6 = (f32[512,256]{1,0:T(8,128)S(1)}, f32[512,256]{1,0:T(8,128)}, u32[]{:S(2)}) copy-start(f32[512,256]{1,0:T(8,128)} %reduce-scatter.2.cloned.1.call-done) | copy-start | bytes 1572868
  104.5 194.9 %all-reduce.6.cloned.1.call-start = ((), (), s32[]{:S(2)}) async-start(), calls=%async_computation.4 | async-start | bytes 262144 | tf_op jit(solution)/shard_map/psum | solution.py:57
  130.8 4.9 %copy-start.3 = (bf16[4096,256]{1,0:T(8,128)(2,1)S(1)}, bf16[4096,256]{1,0:T(8,128)(2,1)}, u32[]{:S(2)}) copy-start(bf16[4096,256]{1,0:T(8,128)(2,1)} %all-gather.2.cloned.1.call-done) | copy-start | bytes 6291460
Sparse Core Ops, SparseCore 0:
  46.2 53.9 reduce-scatter.1
  102.9 27.8 all-gather.1
  137.8 124.9 all-reduce.3
  265.8 33.5 all-reduce.5
where the time goes:
time: 309 us
  waiting for transfers between devices  240 us (78%)
  local copies, waits for them, and re-layouts  30 us (10%)
  matrix products  21 us (7%)
  between operations  13.9 us (4%)
  other arithmetic  3.71 us (1%)
    psum x1, waiting for transfers between devices, body(): grad_head = lax.psum(head_local, ('feat', 'node'))  125 us
    reduce_scatter x1, waiting for transfers between devices, body(): lax.psum_scatter(contract_first(agg_part, w_neigh) + contract_first(own_p...  54.1 us
    psum x1, waiting for transfers between devices, body(): grad_neigh, grad_self = lax.psum((neigh_local, self_local), 'node')  34.7 us
    all_gather x1, waiting for transfers between devices, body(): shard_piece = lax.all_gather(grad_pre, 'feat', axis=0, tiled=True)  26.3 us
    gather x1, local copies, waits for them, and re-layouts, body(): own = jnp.take(feature_rows, target_ids[0], axis=1)  13.8 us
    unnamed x22, local copies, waits for them, and re-layouts  11.6 us
    dot_general x4, matrix products, contract_first(): lax.dot_general(left, right, (((0,), (1,)), ((), ())), preferred_element_...  10.2 us
  transfers between devices with their start and end apart: 4, of which 4 were waited for; matrix products, arithmetic and copies ran while one was open for 4% of the time, Pallas kernels for 0%

commit v1 on v0

--- a/solution.py
+++ b/solution.py
@@ -2,6 +2,22 @@
 import jax.numpy as jnp
 from jax import lax
 from jax.sharding import PartitionSpec as P
+
+
+def row_load(target):
+    s_next, val, v_now = (jax.lax.psum(1, "feat"), jax.lax.axis_index("feat"), target.shape[0])
+    t1, view_out = (target, 1)
+    while view_out < s_next:
+        t1 = jnp.concatenate(
+            [
+                t1,
+                jax.lax.ppermute(t1, "feat", [(k, (k - view_out) % s_next) for k in range(s_next)]),
+            ],
+            axis=0,
+        )
+        view_out = 2 * view_out
+    mid_arr = jnp.roll(t1, val * v_now, axis=0)
+    return mid_arr
 
 
 def aggregate_local(feature_rows, block_row, count_row, adjacency_group):
@@ -49,7 +65,7 @@
     grad_hidden = jnp.dot(cotangent, w_head, preferred_element_type=jnp.float32)
     sigma = jax.nn.sigmoid(preact)
     grad_pre = (grad_hidden * sigma * (1.0 + preact * (1.0 - sigma))).astype(jnp.bfloat16)
-    shard_piece = lax.all_gather(grad_pre, "feat", axis=0, tiled=True)
+    shard_piece = row_load(grad_pre)
     agg_part = aggregate
     own_part = own
     neigh_local = contract_first(shard_piece, agg_part)

time: 309 us -> 296 us (0.958)
  waiting for transfers between devices: 240 us -> 216 us
  local copies, waits for them, and re-layouts: 30 us -> 36.9 us
  starting transfers between devices: 0.16 us -> 4.17 us
    ppermute x0 -> x3, waiting for transfers between devices: none -> 37.5 us  [row_load(): jax.lax.ppermute(t1, 'feat', [(k, (k - view_out) % s_next) for k in range...]
    psum x1, waiting for transfers between devices: 125 us -> 89.4 us  [body(): grad_head = lax.psum(head_local, ('feat', 'node'))]
    all_gather x1 -> x0, waiting for transfers between devices: 26.3 us -> none  [body(): shard_piece = lax.all_gather(grad_pre, 'feat', axis=0, tiled=True)]
    unnamed x22 -> x36, local copies, waits for them, and re-layouts: 11.6 us -> 17.5 us
    ppermute x0 -> x3, starting transfers between devices: none -> 4.05 us  [row_load(): jax.lax.ppermute(t1, 'feat', [(k, (k - view_out) % s_next) for k in range...]
  transfers between devices with their start and end apart: 4 -> 6, of which waited for: 4 -> 6; matrix products, arithmetic and copies ran while one was open for 4% -> 6% of each run, Pallas kernels for 0% -> 0%
where the time goes in v1:
time: 296 us; the launch traced here: 295 us
  waiting for transfers between devices  216 us (73%)
  local copies, waits for them, and re-layouts  36.9 us (12%)
  matrix products  22.4 us (8%)
  between operations  13.9 us (5%)
  starting transfers between devices  4.17 us (1%)
    psum x1, waiting for transfers between devices, body(): grad_head = lax.psum(head_local, ('feat', 'node'))  89.4 us
    reduce_scatter x1, waiting for transfers between devices, body(): lax.psum_scatter(contract_first(agg_part, w_neigh) + contract_first(own_p...  54.1 us
    ppermute x3, waiting for transfers between devices, row_load(): jax.lax.ppermute(t1, 'feat', [(k, (k - view_out) % s_next) for k in range...  37.5 us
    psum x1, waiting for transfers between devices, body(): grad_neigh, grad_self = lax.psum((neigh_local, self_local), 'node')  34.9 us
    unnamed x36, local copies, waits for them, and re-layouts  17.5 us
    gather x1, local copies, waits for them, and re-layouts, body(): own = jnp.take(feature_rows, target_ids[0], axis=1)  13.8 us
    dot_general x4, matrix products, contract_first(): lax.dot_general(left, right, (((0,), (1,)), ((), ())), preferred_element_...  11.7 us
  transfers between devices with their start and end apart: 6, of which 6 were waited for; matrix products, arithmetic and copies ran while one was open for 6% of the time, Pallas kernels for 0%

profile of v1, /device:TPU:0, one launch (start us, length us, event | category | flops | bytes accessed | tf_op | source)
XLA Modules:
  0.0 295.2 jit_solution(17359947115163122103)
XLA Ops:
  8.9 4.8 %copy.26 = bf16[1,64,16384]{1,2,0:T(8,128)(2,1)} copy(bf16[1,64,16384]{2,1,0:T(8,128)(2,1)} %param.9) | data formatting | bytes 4194304 | tf_op args[0]
  14.3 1.4 copy.24
  16.0 13.8 %gather_fusion.1 = bf16[4096,64]{1,0:T(8,128)(2,1)S(1)} fusion(bf16[64,16384]{0,1:T(8,128)(2,1)} %bitcast.57, s32[4096]{0:T(1024)S(1)} %broadcast_clamp_fusion), kind=kCustom, calls=%fused_computation.1 | custom fusion | bytes 1064960 | tf_op jit(solution)/shard_map/jit(_take)/gather | solution.py:49
  29.7 3.1 %gather_fusion = bf16[256,64,128]{2,1,0:T(8,128)(2,1)} fusion(bf16[64,128,128]{2,0,1:T(8,128)(2,1)S(1)} %copy.24, s32[1024]{0:T(1024)S(1)} %pad_clamp_fusion), kind=kCustom, calls=%fused_computation | custom fusion | bytes 8389632 | tf_op jit(solution)/shard_map/jit(_take)/gather | solution.py:28
  32.8 1.4 fusion.32
  35.0 5.6 %fusion.23 = bf16[32,8,8,128]{3,2,1,0:T(8,128)(2,1)S(1)} fusion(bf16[1,32,8,128,128]{4,3,2,1,0:T(8,128)(2,1)} %param.13, bf16[64,32,8,128]{3,0,2,1:T(8,128)(2,1)S(1)} %bitcast.60, pred[32,8]{1,0:T(8,128)(4,1)S(1)} %copy.22, bf16[32,8]{1,0:T(8,128)(2,1)S(1)} %fusion.35, f32[32]{0:T(128)S(1)} %bitcast_convert_fusion), kind=kOutput, calls=%fused_computation.24 | convolution fusion | flops 541589504 | bytes 13108096 | tf_op jit(solution)/shard_map/tkrs,ftks->ftr/dot_general | solution.py:31
  41.4 2.7 convolution_add_fusion
  44.2 54.1 %reduce-scatter.2.cloned.1.call-done = f32[512,256]{1,0:T(8,128)} async-done(((f32[4096,256]{1,0:T(8,128)}), f32[512,256]{1,0:T(8,128)}) %reduce-scatter.2.cloned.1.call-update) | async-done | bytes 524304 | tf_op jit(solution)/shard_map/reduce_scatter | solution.py:52
  98.3 2.0 constant_dynamic-update-slice_fusion.7
  101.3 3.9 %collective-permute-done = bf16[512,256]{1,0:T(8,128)(2,1)S(1)} collective-permute-done((bf16[512,256]{1,0:T(8,128)(2,1)S(1)}, bf16[512,256]{1,0:T(8,128)(2,1)S(1)}, u32[]{:S(2)}, u32[]{:S(2)}) %collective-permute-start) | collective-permute-done | bytes 262176 | tf_op jit(solution)/shard_map/ppermute | solution.py:14
  105.2 1.5 collective-permute-start.1
  106.7 13.0 %collective-permute-done.1 = bf16[1024,256]{1,0:T(8,128)(2,1)S(1)} collective-permute-done((bf16[1024,256]{1,0:T(8,128)(2,1)S(1)}, bf16[1024,256]{1,0:T(8,128)(2,1)S(1)}, u32[]{:S(2)}, u32[]{:S(2)}) %collective-permute-start.1) | collective-permute-done | bytes 524320 | tf_op jit(solution)/shard_map/ppermute | solution.py:14
  120.7 1.7 collective-permute-start.2
  122.4 2.1 convolution_bitcast_fusion
  126.1 20.6 %collective-permute-done.2 = bf16[2048,256]{1,0:T(8,128)(2,1)S(1)} collective-permute-done((bf16[2048,256]{1,0:T(8,128)(2,1)}, bf16[2048,256]{1,0:T(8,128)(2,1)S(1)}, u32[]{:S(2)}, u32[]{:S(2)}) %collective-permute-start.2) | collective-permute-done | bytes 1048608 | tf_op jit(solution)/shard_map/ppermute | solution.py:14
  146.7 1.1 constant_dynamic-update-slice_fusion.4
  150.1 1.1 constant_dynamic-update-slice_fusion
  151.2 4.8 %fusion.7 = f32[256,64]{0,1:T(8,128)} fusion(bf16[8192,256]{1,0:T(8,128)(2,1)} %constant_dynamic-update-slice_fusion, s32[]{:T(128)S(6)} %select_n.62, bf16[4096,64]{1,0:T(8,128)(2,1)S(1)} %gather_fusion.1, pred[4096]{0:T(1024)(128)(4,1)S(1)} %compare_and_fusion), kind=kOutput, calls=%fused_computation.10 | convolution fusion | flops 134479872 | bytes 2691076 | tf_op jit(solution)/shard_map/dot_general | solution.py:39
  155.9 2.7 fusion.9
  159.7 89.4 %all-reduce.4.cloned.1.call-done = f32[256,256]{0,1:T(8,128)} async-done(((f32[256,256]{0,1:T(8,128)}), f32[256,256]{0,1:T(8,128)}) %all-reduce.4.cloned.1.call-update) | async-done | bytes 262160 | tf_op jit(solution)/shard_map/psum | solution.py:64
  249.1 1.8 copy.27
  250.9 34.9 %all-reduce.6.cloned.1.call-done = (f32[256,64]{0,1:T(8,128)}, f32[256,64]{0,1:T(8,128)}) async-done(((f32[256,64]{0,1:T(8,128)}, f32[256,64]{0,1:T(8,128)}), (f32[256,64]{0,1:T(8,128)}, f32[256,64]{0,1:T(8,128)})) %all-reduce.6.cloned.1.call-update) | async-done | bytes 131088 | tf_op jit(solution)/shard_map/psum | solution.py:73
  285.8 1.5 copy.49
  287.2 1.5 copy.50
  (51 shorter events, 11.0 us)
Async XLA Ops:
  7.2 91.2 %copy-start = (bf16[1,512,256]{2,1,0:T(8,128)(2,1)S(1)}, bf16[1,512,256]{2,1,0:T(8,128)(2,1)}, u32[]{:S(2)}) copy-start(bf16[1,512,256]{2,1,0:T(8,128)(2,1)} %param.17) | copy-start | bytes 786436
  7.2 6.5 %copy-start.1 = (bf16[1,64,16384]{2,1,0:T(8,128)(2,1)S(1)}, bf16[1,64,16384]{2,1,0:T(8,128)(2,1)}, u32[]{:S(2)}) copy-start(bf16[1,64,16384]{2,1,0:T(8,128)(2,1)} %param.9) | copy-start | bytes 6291460
  7.2 6.5 %copy-start.5 = (s32[1,4096]{1,0:T(1,128)S(1)}, s32[1,4096]{1,0:T(1,128)}, u32[]{:S(2)}) copy-start(s32[1,4096]{1,0:T(1,128)} %param.10) | copy-start | bytes 49156
  7.2 91.1 %reduce-scatter.2.cloned.1.call-start = ((), (), s32[]{:S(2)}) async-start(), calls=%async_computation.1 | async-start | bytes 4718592 | tf_op jit(solution)/shard_map/reduce_scatter | solution.py:52
  13.7 2.1 copy-start.8
  29.7 3.1 %copy-start.6 = (bf16[256,64]{0,1:T(8,128)(2,1)S(1)}, bf16[256,64]{0,1:T(8,128)(2,1)}, u32[]{:S(2)}) copy-start(bf16[256,64]{0,1:T(8,128)(2,1)} %param.15) | copy-start | bytes 98308
  32.8 2.2 copy-start.2
  35.0 6.5 %copy-start.7 = (bf16[256,64]{0,1:T(8,128)(2,1)S(1)}, bf16[256,64]{0,1:T(8,128)(2,1)}, u32[]{:S(2)}) copy-start(bf16[256,64]{0,1:T(8,128)(2,1)} %param.14) | copy-start | bytes 98308
  40.6 0.8 copy-start.3
  44.1 54.2 %copy-start.10 = (bf16[256,256]{1,0:T(8,128)(2,1)S(1)}, bf16[256,256]{1,0:T(8,128)(2,1)}, u32[]{:S(2)}) copy-start(bf16[256,256]{1,0:T(8,128)(2,1)} %param.16) | copy-start | bytes 393220
  44.2 204.9 %all-reduce.4.cloned.1.call-start = ((), (), s32[]{:S(2)}) async-start(), calls=%async_computation.2 | async-start | bytes 524288 | tf_op jit(solution)/shard_map/psum | solution.py:64
  100.4 4.8 %collective-permute-start = (bf16[512,256]{1,0:T(8,128)(2,1)S(1)}, bf16[512,256]{1,0:T(8,128)(2,1)S(1)}, u32[]{:S(2)}, u32[]{:S(2)}) collective-permute-start(bf16[512,256]{1,0:T(8,128)(2,1)S(1)} %get-tuple-element.19), channel_id=1, source_target_pairs={{0,28},{4,0},{8,4},{12,8},{16,12},{20,16},{24,20},{28,24},{1,29},{... | collective-permute-start | bytes 786440 | tf_op jit(solution)/shard_map/ppermute | solution.py:14
  105.2 14.5 %collective-permute-start.1 = (bf16[1024,256]{1,0:T(8,128)(2,1)S(1)}, bf16[1024,256]{1,0:T(8,128)(2,1)S(1)}, u32[]{:S(2)}, u32[]{:S(2)}) collective-permute-start(bf16[1024,256]{1,0:T(8,128)(2,1)S(1)} %pad_maximum_fusion.1), channel_id=1, source_target_pairs={{0,24},{4,28},{8,0},{12,4},{16,8},{20,12},{24,16},{28,20},{1,25},{... | collective-permute-start | bytes 1572872 | tf_op jit(solution)/shard_map/ppermute | solution.py:14
  120.7 26.0 %collective-permute-start.2 = (bf16[2048,256]{1,0:T(8,128)(2,1)}, bf16[2048,256]{1,0:T(8,128)(2,1)S(1)}, u32[]{:S(2)}, u32[]{:S(2)}) collective-permute-start(bf16[2048,256]{1,0:T(8,128)(2,1)} %pad_maximum_fusion), channel_id=1, source_target_pairs={{0,16},{4,20},{8,24},{12,28},{16,0},{20,4},{24,8},{28,12},{1,17},{... | collective-permute-start | bytes 3145736 | tf_op jit(solution)/shard_map/ppermute | solution.py:14
  124.5 161.3 %all-reduce.6.cloned.1.call-start = ((), (), s32[]{:S(2)}) async-start(), calls=%async_computation.3 | async-start | bytes 262144 | tf_op jit(solution)/shard_map/psum | solution.py:73
  147.8 8.2 %copy-start.4 = (bf16[32,8,8,128]{3,2,1,0:T(8,128)(2,1)S(1)}, bf16[32,8,8,128]{3,2,1,0:T(8,128)(2,1)}, u32[]{:S(2)}) copy-start(bf16[32,8,8,128]{3,2,1,0:T(8,128)(2,1)} %copy-done.3) | copy-start | bytes 1572868
  150.1 8.6 %copy-start.9 = (f32[512,256]{1,0:T(8,128)S(1)}, f32[512,256]{1,0:T(8,128)}, u32[]{:S(2)}) copy-start(f32[512,256]{1,0:T(8,128)} %reduce-scatter.2.cloned.1.call-done) | copy-start | bytes 1572868
  150.1 8.6 %copy-start.11 = (bf16[256,256]{1,0:T(8,128)(2,1)S(1)}, bf16[256,256]{1,0:T(8,128)(2,1)}, u32[]{:S(2)}) copy-start(bf16[256,256]{1,0:T(8,128)(2,1)} %param.16) | copy-start | bytes 393220
Sparse Core Ops, SparseCore 0:
  44.3 53.9 reduce-scatter.1
  124.6 124.4 all-reduce.3
  252.2 33.5 all-reduce.5
